TPU v7x, 512 devices: a whole 4x8x8 slice. The times are simulated.
512 devices in a mesh: ctx: 64 (over z, y), tp: 8 (over x, core).
Axes of the slice: x: 4, y: 8, z: 8, core: 2. Of those that a mesh axis runs over, the one named last changes fastest.
Arguments:
- queries: bfloat16 [32768, 5120], P('ctx', 'tp'), may hold values from -150 to 150
- keys_values: bfloat16 [2, 32768, 1024], P(None, 'ctx', 'tp'), may hold values from -6 to 6
- doc_lengths: int32 [32], replicated, may hold values from 1 to 2049, 32768 in all
- out_weight: bfloat16 [5120, 2560], P('tp'), may hold values from -0.078125 to 0.078125
Outputs:
- mixed: bfloat16 [32768, 2560], P(('ctx', 'tp'))
Inputs may be any that keep to these rules, and one draw needn't show every extreme that they name: `doc_lengths`: the lengths sum to 32768; none exceeds 2049, and one equals 2049.
All inputs are finite; a program needn't handle non-finite values.
Results may differ from a plain program's by a relative error of at most 0.018.
Values may be sent and summed in bfloat16 or wider, within the bound.
A program may use at most 64 MiB of HBM per device.

v0:
```python
import math

import jax
import jax.numpy as jnp
from jax import lax
from jax.sharding import PartitionSpec as P

HEADS = 40
KV_HEADS = 8
HEAD_DIM = 128
SPAN = 4


def from_behind(array, axis, by):
    size = lax.axis_size(axis)
    pairs = [(i, i + by) for i in range(size) if 0 <= i + by < size]
    return lax.ppermute(array, axis, pairs)


def on_device(queries, keys_values, doc_lengths, out_weight):
    rows_here = queries.shape[0]
    device_index = lax.axis_index("ctx")
    kv_width = keys_values.shape[2]
    local_kv = kv_width // HEAD_DIM
    group_size = HEADS // KV_HEADS
    score_scale = 1.0 / math.sqrt(HEAD_DIM)
    doc_ends = jnp.cumsum(doc_lengths)
    local_rows = jnp.arange(rows_here, dtype=jnp.int32)

    def doc_of(positions):
        return jnp.sum((positions[:, None] >= doc_ends[None, :]).astype(jnp.int32), axis=1)

    query_pos = device_index * rows_here + local_rows
    query_doc = doc_of(query_pos)
    query_heads = queries.reshape(rows_here, local_kv, group_size, HEAD_DIM)
    kv_blocks = [keys_values]
    for offset in range(1, SPAN + 1):
        kv_blocks.append(from_behind(keys_values, "ctx", offset))

    def live_mask(offset):
        key_pos = (device_index - offset) * rows_here + local_rows
        key_doc = doc_of(key_pos)
        return (
            (query_doc[:, None] == key_doc[None, :])
            & (key_pos[None, :] <= query_pos[:, None])
            & (key_pos[None, :] >= 0)
        )

    def attend(carried, kv_block, allowed):
        max_old, total_old, accumulated = carried
        key_heads = kv_block[0].reshape(rows_here, local_kv, HEAD_DIM)
        value_heads = kv_block[1].reshape(rows_here, local_kv, HEAD_DIM)
        scores = (
            jnp.einsum("qkgd,skd->qkgs", query_heads, key_heads, preferred_element_type=jnp.float32)
            * score_scale
        )
        scores = jnp.where(allowed[:, None, None, :], scores, jnp.float32(-1e30))
        max_new = jnp.maximum(max_old, jnp.max(scores, axis=-1))
        factor = jnp.exp(max_old - max_new)
        weights = jnp.exp(scores - max_new[..., None])
        total_new = total_old * factor + jnp.sum(weights, axis=-1)
        accumulated = accumulated * factor[..., None] + jnp.einsum(
            "qkgs,skd->qkgd",
            weights.astype(jnp.bfloat16),
            value_heads,
            preferred_element_type=jnp.float32,
        )
        return (max_new, total_new, accumulated)

    carried = (
        jnp.full((rows_here, local_kv, group_size), -1e30, jnp.float32),
        jnp.zeros((rows_here, local_kv, group_size), jnp.float32),
        jnp.zeros((rows_here, local_kv, group_size, HEAD_DIM), jnp.float32),
    )
    carried = attend(carried, kv_blocks[0], live_mask(0))
    for offset in range(1, SPAN + 1):
        allowed = live_mask(offset)
        carried = attend(carried, kv_blocks[offset], allowed)
    max_all, total_all, accumulated = carried
    attended = (
        (accumulated / total_all[..., None])
        .reshape(rows_here, local_kv * group_size * HEAD_DIM)
        .astype(jnp.bfloat16)
    )
    return lax.psum_scatter(
        jnp.dot(attended, out_weight, preferred_element_type=jnp.float32).astype(jnp.bfloat16),
        "tp",
        scatter_dimension=0,
        tiled=True,
    )


def solution(mesh):
    placed = (P("ctx", "tp"), P(None, "ctx", "tp"), P(), P("tp", None))
    return jax.shard_map(
        on_device, mesh=mesh, in_specs=placed, out_specs=P(("ctx", "tp"), None), check_vma=False
    )
```

profile of v0, /device:TPU:8, one launch (start us, length us, event | category | flops | bytes accessed | tf_op | source)
XLA Modules:
  0.0 136.9 jit_solution(2412319307311908182)
XLA Ops:
  6.5 0.0 copy-start
  6.5 0.0 reduce-scatter.2.cloned.1.call-start
  6.5 5.5 %collective-permute-start.1 = (bf16[2,512,128]{2,1,0:T(8,128)(2,1)}, bf16[2,512,128]{2,1,0:T(8,128)(2,1)}, u32[]{:S(2)}, u32[]{:S(2)}) collective-permute-start(bf16[2,512,128]{2,1,0:T(8,128)(2,1)} %param.5), channel_id=1, source_target_pairs={{0,16},{8,24},{16,32},{24,40},{32,48},{40,56},{48,64},{56,72},{64,... | collective-permute-start | bytes 786440 | tf_op jit(solution)/shard_map/ppermute | solution.py:17
  12.0 4.0 %collective-permute-start = (bf16[2,512,128]{2,1,0:T(8,128)(2,1)}, bf16[2,512,128]{2,1,0:T(8,128)(2,1)S(1)}, u32[]{:S(2)}, u32[]{:S(2)}) collective-permute-start(bf16[2,512,128]{2,1,0:T(8,128)(2,1)} %param.5), channel_id=1, source_target_pairs={{0,8},{8,16},{16,24},{24,32},{32,40},{40,48},{48,56},{56,64},{64,7... | collective-permute-start | bytes 786440 | tf_op jit(solution)/shard_map/ppermute | solution.py:17
  16.0 4.5 %collective-permute-start.3 = (bf16[2,512,128]{2,1,0:T(8,128)(2,1)}, bf16[2,512,128]{2,1,0:T(8,128)(2,1)}, u32[]{:S(2)}, u32[]{:S(2)}) collective-permute-start(bf16[2,512,128]{2,1,0:T(8,128)(2,1)} %param.5), channel_id=1, source_target_pairs={{0,32},{8,40},{16,48},{24,56},{32,64},{40,72},{48,80},{56,88},{64,... | collective-permute-start | bytes 786440 | tf_op jit(solution)/shard_map/ppermute | solution.py:17
  20.5 5.5 %collective-permute-start.2 = (bf16[2,512,128]{2,1,0:T(8,128)(2,1)}, bf16[2,512,128]{2,1,0:T(8,128)(2,1)}, u32[]{:S(2)}, u32[]{:S(2)}) collective-permute-start(bf16[2,512,128]{2,1,0:T(8,128)(2,1)} %param.5), channel_id=1, source_target_pairs={{0,24},{8,32},{16,40},{24,48},{32,56},{40,64},{48,72},{56,80},{64,... | collective-permute-start | bytes 786440 | tf_op jit(solution)/shard_map/ppermute | solution.py:17
  26.1 0.5 broadcast_compare_fusion.4
  26.6 0.6 iota_add_fusion.4
  27.2 0.5 broadcast_compare_fusion
  27.7 0.6 iota_add_fusion
  28.3 0.6 broadcast_compare_fusion.2
  28.9 0.6 iota_add_fusion.2
  29.5 1.3 copy.38
  30.8 0.8 reduce-window.8
  31.6 0.6 reduce.10
  32.2 2.2 %copy.39 = bf16[512,640]{0,1:T(8,128)(2,1)} copy(bf16[512,640]{1,0:T(8,128)(2,1)} %param.4) | data formatting | bytes 1310720 | tf_op args[0]
  34.4 0.0 copy-start.1
  34.4 0.9 convert_reduce_fusion
  35.3 2.6 %and_and_fusion.4 = (pred[512,512]{0,1:T(8,128)(4,1)S(1)}, pred[512,512]{0,1:T(8,128)(4,1)S(1)}, pred[512,512]{0,1:T(8,128)(4,1)S(1)}, pred[512,512]{0,1:T(8,128)(4,1)S(1)}, pred[512,512]{0,1:T(8,128)(4,1)S(1)}) fusion(s32[512]{0:T(512)} %iota_add_fusion.4, s32[512]{0:T(512)S(1)} %get-tuple-element.9, pred[512]{0:T(512)(128)(4,1)} %broadcast_compare_fusion.4, ...), kind=kLoop, calls=%fused_computation.60 | loop fusion | flops 5242880 | bytes 1333760 | tf_op jit(solution)/shard_map/and | solution.py:44
  37.8 2.2 %fusion.10 = (f32[512,5]{0,1:T(8,128)S(1)}, f32[512,512,5]{1,0,2:T(8,128)S(1)}) fusion(pred[512,512]{0,1:T(8,128)(4,1)S(1)} %get-tuple-element.21, bf16[512,5,128]{0,2,1:T(8,128)(2,1)} %bitcast.247, bf16[2,512,128]{2,1,0:T(8,128)(2,1)} %param.5), kind=kOutput, calls=%fused_computation.21 | convolution fusion | flops 339473920 | bytes 6301696 | tf_op jit(solution)/shard_map/qkgd,skd->qkgs/dot_general | solution.py:54
  40.0 16.3 %collective-permute-done.2 = bf16[2,512,128]{2,1,0:T(8,128)(2,1)} collective-permute-done((bf16[2,512,128]{2,1,0:T(8,128)(2,1)}, bf16[2,512,128]{2,1,0:T(8,128)(2,1)}, u32[]{:S(2)}, u32[]{:S(2)}) %collective-permute-start.2) | collective-permute-done | bytes 262176 | tf_op jit(solution)/shard_map/ppermute | solution.py:17
  56.4 0.0 copy-done.1
  56.4 2.0 %fusion.13 = (f32[512,5]{0,1:T(8,128)S(1)}, f32[512,512,5]{1,0,2:T(8,128)S(1)}) fusion(pred[512,512]{0,1:T(8,128)(4,1)S(1)} %get-tuple-element.22, bf16[512,5,128]{0,2,1:T(8,128)(2,1)S(1)} %bitcast.248, bf16[2,512,128]{2,1,0:T(8,128)(2,1)} %collective-permute-done.2), kind=kOutput, calls=%fused_computation.24 | convolution fusion | flops 339473920 | bytes 6301696 | tf_op jit(solution)/shard_map/qkgd,skd->qkgs/dot_general | solution.py:54
  58.3 0.0 collective-permute-done.3
  58.4 2.0 %fusion.14 = (f32[512,5]{0,1:T(8,128)S(1)}, f32[512,512,5]{1,0,2:T(8,128)S(1)}) fusion(pred[512,512]{0,1:T(8,128)(4,1)S(1)} %get-tuple-element.23, bf16[512,5,128]{0,2,1:T(8,128)(2,1)S(1)} %bitcast.249, bf16[2,512,128]{2,1,0:T(8,128)(2,1)} %collective-permute-done.3), kind=kOutput, calls=%fused_computation.25 | convolution fusion | flops 339473920 | bytes 6301696 | tf_op jit(solution)/shard_map/qkgd,skd->qkgs/dot_general | solution.py:54
  60.3 0.0 collective-permute-done.1
  60.3 2.0 %fusion.12 = (f32[512,5]{0,1:T(8,128)S(1)}, f32[512,512,5]{1,0,2:T(8,128)S(1)}) fusion(pred[512,512]{0,1:T(8,128)(4,1)S(1)} %get-tuple-element.24, bf16[512,5,128]{0,2,1:T(8,128)(2,1)S(1)} %bitcast.250, bf16[2,512,128]{2,1,0:T(8,128)(2,1)} %collective-permute-done.1), kind=kOutput, calls=%fused_computation.23 | convolution fusion | flops 339473920 | bytes 6301696 | tf_op jit(solution)/shard_map/qkgd,skd->qkgs/dot_general | solution.py:54
  62.3 0.0 collective-permute-done
  62.3 1.0 fusion.11
  63.4 1.1 fusion
  64.5 1.1 fusion.8
  65.6 1.1 fusion.6
  66.7 0.0 copy-start.2
  66.7 1.1 fusion.4
  67.8 1.1 fusion.2
  69.0 0.0 copy-done.2
  69.0 1.7 %fusion.53 = f32[1,128,512,5]{2,1,3,0:T(8,128)S(1)} fusion(f32[512,512,5]{1,0,2:T(8,128)S(1)} %get-tuple-element.35, f32[512,5]{0,1:T(8,128)S(1)} %get-tuple-element.20, pred[512,512]{0,1:T(8,128)(4,1)S(1)} %get-tuple-element.21, f32[512,5]{0,1:T(8,128)S(1)} %get-tuple-element.14, f32[512,5]{0,1:T(8,128)S(1)} %get-tuple-element.19, ...), kind=kOutput, calls=%fused_computation.47 | convolution fusion | flops 341442560 | bytes 6995968 | tf_op jit(solution)/shard_map/qkgs,skd->qkgd/dot_general | solution.py:62
  70.7 2.3 %fusion.35 = f32[1,128,512,5]{2,1,3,0:T(8,128)S(1)} fusion(f32[512,512,5]{1,0,2:T(8,128)S(1)} %get-tuple-element.27, f32[512,5]{0,1:T(8,128)S(1)} %get-tuple-element.15, pred[512,512]{0,1:T(8,128)(4,1)S(1)} %get-tuple-element.23, bf16[2,512,128]{2,1,0:T(8,128)(2,1)} %collective-permute-done.3), kind=kOutput, calls=%fused_computation.41 | convolution fusion | flops 340787200 | bytes 6957056 | tf_op jit(solution)/shard_map/qkgs,skd->qkgd/dot_general | solution.py:62
  73.0 2.3 %fusion.38 = f32[1,128,512,5]{2,1,3,0:T(8,128)S(1)} fusion(f32[512,512,5]{1,0,2:T(8,128)S(1)} %get-tuple-element.29, f32[512,5]{0,1:T(8,128)S(1)} %get-tuple-element.16, pred[512,512]{0,1:T(8,128)(4,1)S(1)} %get-tuple-element.22, bf16[2,512,128]{2,1,0:T(8,128)(2,1)} %collective-permute-done.2), kind=kOutput, calls=%fused_computation.42 | convolution fusion | flops 340787200 | bytes 6957056 | tf_op jit(solution)/shard_map/qkgs,skd->qkgd/dot_general | solution.py:62
  75.4 2.3 %fusion.41 = f32[1,128,512,5]{2,1,3,0:T(8,128)S(1)} fusion(f32[512,512,5]{1,0,2:T(8,128)S(1)} %get-tuple-element.31, f32[512,5]{0,1:T(8,128)S(1)} %get-tuple-element.17, pred[512,512]{0,1:T(8,128)(4,1)S(1)} %get-tuple-element.24, bf16[2,512,128]{2,1,0:T(8,128)(2,1)} %collective-permute-done.1), kind=kOutput, calls=%fused_computation.43 | convolution fusion | flops 340787200 | bytes 6957056 | tf_op jit(solution)/shard_map/qkgs,skd->qkgd/dot_general | solution.py:62
  77.7 1.8 %divide_convert_fusion = bf16[1,128,512,5]{2,1,3,0:T(8,128)(2,1)S(1)} fusion(f32[1,128,512,5]{2,1,3,0:T(8,128)S(1)} %fusion.35, f32[1,128,512,5]{2,1,3,0:T(8,128)S(1)} %fusion.38, f32[1,128,512,5]{2,1,3,0:T(8,128)S(1)} %fusion.41, f32[1,128,512,5]{2,1,3,0:T(8,128)S(1)} %fusion.53, f32[512,512,5]{1,0,2:T(8,128)S(1)} %get-tuple-element.33, ...), kind=kOutput, calls=%fused_computation.55 | convolution fusion | flops 343736320 | bytes 11616256 | tf_op jit(solution)/shard_map/qkgs,skd->qkgd/dot_general | solution.py:62
  79.4 0.0 copy-done
  79.5 3.7 %convolution_convert_fusion = bf16[512,2560]{1,0:T(8,128)(2,1)} fusion(bf16[512,640]{0,1:T(8,128)(2,1)S(1)} %bitcast.252, bf16[640,2560]{1,0:T(8,128)(2,1)S(1)} %copy-done), kind=kOutput, calls=%fused_computation.20 | convolution fusion | flops 1679032320 | bytes 6553600 | tf_op jit(solution)/shard_map/dot_general | solution.py:86
  83.2 0.0 reduce-scatter.2.cloned.1.call-update
  83.2 46.8 %reduce-scatter.2.cloned.1.call-done = bf16[64,2560]{1,0:T(8,128)(2,1)} async-done(((bf16[512,2560]{1,0:T(8,128)(2,1)}), bf16[64,2560]{1,0:T(8,128)(2,1)}) %reduce-scatter.2.cloned.1.call-update) | async-done | bytes 327696 | tf_op jit(solution)/shard_map/reduce_scatter | solution.py:85
  (2 shorter events, 0.1 us)
Async XLA Ops:
  6.5 72.9 %copy-start = (bf16[640,2560]{1,0:T(8,128)(2,1)S(1)}, bf16[640,2560]{1,0:T(8,128)(2,1)}, u32[]{:S(2)}) copy-start(bf16[640,2560]{1,0:T(8,128)(2,1)} %param.7) | copy-start | bytes 9830404
  6.5 123.5 %reduce-scatter.2.cloned.1.call-start = ((), (), s32[]{:S(2)}) async-start(), calls=%async_computation.1 | async-start | bytes 2949120 | tf_op jit(solution)/shard_map/reduce_scatter | solution.py:85
  6.5 53.8 %collective-permute-start.1 = (bf16[2,512,128]{2,1,0:T(8,128)(2,1)}, bf16[2,512,128]{2,1,0:T(8,128)(2,1)}, u32[]{:S(2)}, u32[]{:S(2)}) collective-permute-start(bf16[2,512,128]{2,1,0:T(8,128)(2,1)} %param.5), channel_id=1, source_target_pairs={{0,16},{8,24},{16,32},{24,40},{32,48},{40,56},{48,64},{56,72},{64,... | collective-permute-start | bytes 786440 | tf_op jit(solution)/shard_map/ppermute | solution.py:17
  12.0 50.3 %collective-permute-start = (bf16[2,512,128]{2,1,0:T(8,128)(2,1)}, bf16[2,512,128]{2,1,0:T(8,128)(2,1)S(1)}, u32[]{:S(2)}, u32[]{:S(2)}) collective-permute-start(bf16[2,512,128]{2,1,0:T(8,128)(2,1)} %param.5), channel_id=1, source_target_pairs={{0,8},{8,16},{16,24},{24,32},{32,40},{40,48},{48,56},{56,64},{64,7... | collective-permute-start | bytes 786440 | tf_op jit(solution)/shard_map/ppermute | solution.py:17
  16.0 42.3 %collective-permute-start.3 = (bf16[2,512,128]{2,1,0:T(8,128)(2,1)}, bf16[2,512,128]{2,1,0:T(8,128)(2,1)}, u32[]{:S(2)}, u32[]{:S(2)}) collective-permute-start(bf16[2,512,128]{2,1,0:T(8,128)(2,1)} %param.5), channel_id=1, source_target_pairs={{0,32},{8,40},{16,48},{24,56},{32,64},{40,72},{48,80},{56,88},{64,... | collective-permute-start | bytes 786440 | tf_op jit(solution)/shard_map/ppermute | solution.py:17
  20.5 35.8 %collective-permute-start.2 = (bf16[2,512,128]{2,1,0:T(8,128)(2,1)}, bf16[2,512,128]{2,1,0:T(8,128)(2,1)}, u32[]{:S(2)}, u32[]{:S(2)}) collective-permute-start(bf16[2,512,128]{2,1,0:T(8,128)(2,1)} %param.5), channel_id=1, source_target_pairs={{0,24},{8,32},{16,40},{24,48},{32,56},{40,64},{48,72},{56,80},{64,... | collective-permute-start | bytes 786440 | tf_op jit(solution)/shard_map/ppermute | solution.py:17
  34.4 22.0 %copy-start.1 = (bf16[512,640]{0,1:T(8,128)(2,1)S(1)}, bf16[512,640]{0,1:T(8,128)(2,1)}, u32[]{:S(2)}) copy-start(bf16[512,640]{0,1:T(8,128)(2,1)} %copy.39) | copy-start | bytes 1966084
  66.7 2.3 %copy-start.2 = (bf16[2,512,128]{2,1,0:T(8,128)(2,1)S(1)}, bf16[2,512,128]{2,1,0:T(8,128)(2,1)}, u32[]{:S(2)}) copy-start(bf16[2,512,128]{2,1,0:T(8,128)(2,1)} %param.5) | copy-start | bytes 786436
Sparse Core Ops, SparseCore 0:
  83.3 46.6 reduce-scatter.1
where the time goes:
time: 137 us
  waiting for transfers between devices  63.2 us (46%)
  matrix products  23.2 us (17%)
  starting transfers between devices  19.5 us (14%)
  other arithmetic  13.8 us (10%)
  between operations  13.6 us (10%)
  local copies, waits for them, and re-layouts  3.52 us (3%)
    reduce_scatter x1, waiting for transfers between devices, on_device(): lax.psum_scatter(jnp.dot(attended, out_weight, preferred_element_type=jnp...  46.8 us
    ppermute x4, starting transfers between devices, from_behind(): return lax.ppermute(array, axis, pairs)  19.5 us
    ppermute x4, waiting for transfers between devices, from_behind(): return lax.ppermute(array, axis, pairs)  16.4 us
    dot_general x5, matrix products, attend(): jnp.einsum('qkgs,skd->qkgd', weights.astype(jnp.bfloat16), value_heads, p...  10.4 us
    dot_general x5, matrix products, attend(): jnp.einsum('qkgd,skd->qkgs', query_heads, key_heads, preferred_element_ty...  9.09 us
    reduce_sum x5, other arithmetic, attend(): total_new = total_old * factor + jnp.sum(weights, axis=-1)  5.52 us
    dot_general x1, matrix products, on_device(): jnp.dot(attended, out_weight, preferred_element_type=jnp.float32)  3.74 us
  transfers between devices with their start and end apart: 5, of which 2 were waited for; matrix products, arithmetic and copies ran while one was open for 14% of the time, Pallas kernels for 0%

commit v1 on v0

v1 whole, which is shorter than its diff:
```python
import math

import jax
import jax.numpy as jnp
from jax import lax
from jax.experimental import pallas as pl
from jax.experimental.pallas import tpu as pltpu
from jax.sharding import PartitionSpec as P

HEAD_DIM = 128
SPAN = 4
TILE = 128
LOW = -(2.0**100)
LOGICAL = pl.DeviceIdType.MESH
FAR = 3


def kernel(
    doc_ref, q_hbm, kv_hbm, w_hbm, out_ref,
    qs, qe, ke, kvb, relay, top, acc, att, att_sib, wbuf, pbuf, step_in, fwd, near, last, mine,
    q_sem, kv_sem, w_sem,
    up_send, up_recv, down_send, down_recv, w_send, w_recv, att_send, att_recv,
    s1_send, s1_recv, near_send, near_recv, last_send, last_recv, mine_send, mine_recv,
):
    n_ctx = lax.axis_size("ctx")
    n_rows = kvb.shape[2]
    n_tiles = n_rows // TILE
    heads = qs.shape[1] // TILE
    docs = doc_ref.shape[0]
    half_cols = pbuf.shape[3]
    me = lax.axis_index("ctx")
    tp = lax.axis_index("tp")
    x = tp // 2
    core = tp % 2
    x1 = x + 1 - 2 * (x % 2)
    x2 = (x + 2) % 4
    x3 = 3 - x
    up = (me + 1) % n_ctx
    down = (me + n_ctx - 1) % n_ctx
    jump = (me + 5) % n_ctx
    back = (me + n_ctx - 5) % n_ctx
    sib = x * 2 + 1 - core

    barrier = pltpu.get_barrier_semaphore()
    friends = [(up, tp), (down, tp), (jump, tp), (back, tp), (me, sib)]
    friends += [(me, x1 * 2 + k) for k in range(2)] + [(me, x3 * 2 + k) for k in range(2)]
    for friend in friends:
        pl.semaphore_signal(barrier, inc=1, device_id=friend, device_id_type=LOGICAL)

    q_copies = [
        pltpu.make_async_copy(
            q_hbm.at[:, :, pl.ds(h * HEAD_DIM, HEAD_DIM)],
            qs.at[:, pl.ds(h * TILE, TILE), :],
            q_sem.at[h],
        )
        for h in range(heads)
    ]
    kv_copy = pltpu.make_async_copy(kv_hbm, kvb.at[0], kv_sem)
    my_cols = pl.ds(pl.multiple_of(core * 2 * half_cols, 128), 2 * half_cols)
    sib_cols = pl.ds(pl.multiple_of((1 - core) * 2 * half_cols, 128), 2 * half_cols)
    w_copy = pltpu.make_async_copy(w_hbm.at[:, my_cols], wbuf.at[0], w_sem)
    kv_copy.start()
    for c in q_copies:
        c.start()

    def remote(src, dst, send, recv, to):
        return pltpu.make_async_remote_copy(
            src_ref=src, dst_ref=dst, send_sem=send, recv_sem=recv, device_id=to, device_id_type=LOGICAL
        )

    def piece(ref, c):
        return ref.at[:, pl.ds(c * TILE, TILE), :]

    def up_copy(j, c):
        src = piece(kv_hbm if j == 1 else kvb.at[j - 1], c)
        return remote(src, piece(kvb.at[j], c), up_send.at[j - 1, c], up_recv.at[j - 1, c], (up, tp))

    def down_copy(j):
        if j == 5:
            return remote(piece(kv_hbm, FAR), relay, down_send.at[4], down_recv.at[4], (jump, tp))
        src = relay if j == 4 else piece(kvb.at[j + 1], FAR)
        return remote(src, piece(kvb.at[j], FAR), down_send.at[j - 1], down_recv.at[j - 1], (down, tp))

    w_remote = remote(w_hbm.at[:, sib_cols], wbuf.at[1], w_send, w_recv, (me, sib))

    lane = lax.broadcasted_iota(jnp.int32, (1, 128), 1)
    low_end = jnp.zeros((1, 128), jnp.int32)
    high_end = jnp.zeros((1, 128), jnp.int32)
    end = jnp.int32(0)
    for d in range(docs):
        low_end = jnp.where(lane == d, end, low_end)
        end = end + doc_ref[d]
        high_end = jnp.where(lane == d, end, high_end)
    row = lax.broadcasted_iota(jnp.int32, (n_rows, 128), 0)

    def inside(offset):
        pos = row + (me - offset) * n_rows
        return (pos >= low_end) & (pos < high_end)

    qe[...] = jnp.where(inside(0), 1.0, 0.0).astype(jnp.bfloat16).reshape(qe.shape)
    ke[0] = jnp.where(inside(0), 0.0, LOW).astype(jnp.bfloat16)

    pl.semaphore_wait(barrier, len(friends))
    ups, downs = {}, {}
    order = list(range(FAR))[::-1]
    for c in order:
        ups[1, c] = up_copy(1, c)
        ups[1, c].start()
    downs[5] = down_copy(5)
    downs[5].start()
    w_remote.start()
    w_copy.start()

    for j in range(1, SPAN + 1):
        ke[j] = jnp.where(inside(j), 0.0, LOW).astype(jnp.bfloat16)

    def got_up(j, c):
        ups[j, c].wait_recv()
        if j < SPAN:
            ups[j + 1, c] = up_copy(j + 1, c)
            ups[j + 1, c].start()

    def got_down(j):
        downs[j].wait_recv()
        if j > 1:
            downs[j - 1] = down_copy(j - 1)
            downs[j - 1].start()

    scale = math.log2(math.e) / math.sqrt(HEAD_DIM)

    def keys_of(spans):
        k = jnp.concatenate([kvb[j, 0, r : r + n, :] for j, r, n in spans], axis=0)
        e = jnp.concatenate([ke[j, r : r + n, :] for j, r, n in spans], axis=0)
        return jnp.concatenate([k, e], axis=1)

    def values_of(spans):
        v = jnp.concatenate([kvb[j, 1, r : r + n, :] for j, r, n in spans], axis=0)
        return jnp.concatenate([v, jnp.ones_like(v)], axis=1)

    def scores(item):
        t, spans, first = item
        q = jnp.concatenate([qs[t], jnp.concatenate([qe[t]] * heads, axis=0)], axis=1)
        s = lax.dot_general(q, keys_of(spans), (((1,), (1,)), ((), ())), preferred_element_type=jnp.float32)
        if first:
            n = s.shape[1]
            shape = (TILE * heads, TILE)
            key = lax.broadcasted_iota(jnp.int32, shape, 1)
            query = lax.broadcasted_iota(jnp.int32, (heads, TILE, TILE), 1).reshape(shape)
            own = jnp.where(key <= query, s[:, n - TILE :], LOW)
            s = own if n == TILE else jnp.concatenate([s[:, : n - TILE], own], axis=1)
        return s

    def soften(item, s):
        t, _, first = item
        copies = s.shape[1] // 128
        most = jnp.broadcast_to(jnp.max(s, axis=1, keepdims=True), (s.shape[0], 128))
        if first:
            factor = None
        else:
            before = top[t]
            most = jnp.maximum(before, most)
            factor = jnp.exp2((before - most) * scale)
        weights = jnp.exp2((s - jnp.concatenate([most] * copies, axis=1)) * scale).astype(jnp.bfloat16)
        top[t] = most
        return weights, factor

    def gather(item, weights, factor):
        t, spans, first = item
        part = jnp.dot(weights, values_of(spans), preferred_element_type=jnp.float32)
        if first:
            acc[t] = part
        else:
            acc[t] = acc[t] * jnp.concatenate([factor, factor], axis=1) + part

    def attend(items):
        held = scores(items[0])
        pending = None
        for i, item in enumerate(items):
            following = scores(items[i + 1]) if i + 1 < len(items) else None
            now = soften(item, held)
            if pending is not None:
                gather(*pending)
            pending = (item, *now)
            held = following
        gather(*pending)

    kv_copy.wait()
    for c in q_copies:
        c.wait()
    attend([(t, [(0, 0, (t + 1) * TILE)], True) for t in range(n_tiles)])

    def block(n):
        return [(n, 0, FAR * TILE), (5 - n, FAR * TILE, TILE)]

    got_up(1, 2)
    got_up(1, 1)
    got_up(1, 0)
    got_down(5)
    got_up(2, 2)
    got_down(4)
    attend([(t, block(1), False) for t in (0, 1)])
    got_up(2, 1)
    attend([(t, block(1), False) for t in (2, 3)])
    got_up(2, 0)
    got_up(3, 2)
    got_down(3)
    attend([(t, block(2), False) for t in (0, 1)])
    got_up(3, 1)
    attend([(t, block(2), False) for t in (2, 3)])
    got_up(3, 0)
    got_down(2)
    attend([(t, block(3), False) for t in (0, 1)])
    got_up(4, 2)
    attend([(t, block(3), False) for t in (2, 3)])
    got_up(4, 1)
    got_down(1)
    lasts = []
    for t in (3, 2, 1, 0):
        spans = [(1, FAR * TILE, TILE)]
        first_row = max(t, 1) * TILE
        if first_row < FAR * TILE:
            spans = [(4, first_row, FAR * TILE - first_row)] + spans
        lasts.append((t, spans, False))
    attend(lasts)
    got_up(4, 0)
    attend([(0, [(4, 0, TILE)], False)])

    att_copies = {}
    for place, t in enumerate((x2, x1, x3, x)):
        a = acc[t]
        whole = (a[:, :HEAD_DIM] / a[:, HEAD_DIM:]).astype(jnp.bfloat16)
        for h in range(heads):
            att[place, :, h * HEAD_DIM : (h + 1) * HEAD_DIM] = whole[h * TILE : (h + 1) * TILE, :]
        att_copies[place] = remote(
            att.at[place], att_sib.at[place], att_send.at[place], att_recv.at[place], (me, sib)
        )
        att_copies[place].start()

    w_copy.wait()
    w_remote.wait()
    sends = []

    def project(place):
        att_copies[place].wait()
        for side in range(2):
            cols = slice(side * half_cols, (side + 1) * half_cols)
            part = jnp.dot(att[place], wbuf[0, :, cols], preferred_element_type=jnp.float32)
            part = part + jnp.dot(att_sib[place], wbuf[1, :, cols], preferred_element_type=jnp.float32)
            pbuf[place, side] = part.astype(jnp.bfloat16)

    def send(copy):
        copy.start()
        sends.append(copy)
        return copy

    rows_out = TILE // 2
    partner = (x1, x3)

    def to_cores(src, dst, send_sem, recv_sem, side, chip):
        for k in range(2):
            send(
                remote(
                    src.at[pl.ds(k * rows_out, rows_out), :],
                    dst.at[core, side],
                    send_sem.at[side, k],
                    recv_sem.at[core, side],
                    (me, chip * 2 + k),
                )
            )

    project(0)
    hops = [
        send(remote(pbuf.at[0, side], step_in.at[side], s1_send.at[side], s1_recv.at[side], (me, partner[side] * 2 + core)))
        for side in range(2)
    ]
    project(1)
    to_cores(pbuf.at[1, 0], near, near_send, near_recv, 0, x1)
    project(2)
    to_cores(pbuf.at[2, 1], near, near_send, near_recv, 1, x3)
    project(3)
    other = pl.multiple_of((1 - core) * rows_out, rows_out)
    own = pl.multiple_of(core * rows_out, rows_out)
    mine_copy = send(
        remote(pbuf.at[3, :, pl.ds(other, rows_out), :], mine, mine_send, mine_recv, (me, sib))
    )
    for side in range(2):
        hops[side].wait_recv()
        held = pbuf[2 - side, side].astype(jnp.float32) + step_in[side].astype(jnp.float32)
        fwd[side] = held.astype(jnp.bfloat16)
        to_cores(fwd.at[side], last, last_send, last_recv, side, partner[1 - side])

    def arrived(buf, sems_s, sems_r, k, side):
        remote(buf.at[k, side], buf.at[k, side], sems_s.at[side, 0], sems_r.at[k, side], (me, sib)).wait_recv()

    mine_copy.wait_recv()
    for k in range(2):
        for side in range(2):
            arrived(near, near_send, near_recv, k, side)
    for side in range(2):
        for k in range(2):
            arrived(last, last_send, last_recv, k, side)
            here = pbuf[3, side, pl.ds(own, rows_out), :].astype(jnp.float32)
            there = mine[side].astype(jnp.float32)
            base = jnp.where(core == k, here, there)
            total = base + near[k, side].astype(jnp.float32) + last[k, side].astype(jnp.float32)
            col = (2 * k + side) * half_cols
            out_ref[:, col : col + half_cols] = total.astype(jnp.bfloat16)

    for copy in sends:
        copy.wait_send()
    for copy in ups.values():
        copy.wait_send()
    for copy in downs.values():
        copy.wait_send()


def on_device(queries, keys_values, doc_lengths, out_weight):
    rows, width = queries.shape
    cols = out_weight.shape[1]
    heads = width // HEAD_DIM
    tiles = rows // TILE
    half = cols // 4
    n_tp = lax.axis_size("tp")
    bf, f32 = jnp.bfloat16, jnp.float32
    dma = pltpu.SemaphoreType.DMA
    hbm = pl.BlockSpec(memory_space=pl.ANY)
    return pl.pallas_call(
        kernel,
        out_shape=jax.ShapeDtypeStruct((rows // n_tp, cols), bf),
        in_specs=[pl.BlockSpec(memory_space=pltpu.SMEM), hbm, hbm, hbm],
        out_specs=pl.BlockSpec(memory_space=pltpu.VMEM),
        scratch_shapes=[
            pltpu.VMEM((tiles, heads * TILE, HEAD_DIM), bf),
            pltpu.VMEM((tiles, TILE, 128), bf),
            pltpu.VMEM((SPAN + 1, rows, 128), bf),
            pltpu.VMEM((SPAN + 1, 2, rows, HEAD_DIM), bf),
            pltpu.VMEM((2, TILE, HEAD_DIM), bf),
            pltpu.VMEM((tiles, heads * TILE, 128), f32),
            pltpu.VMEM((tiles, heads * TILE, 2 * HEAD_DIM), f32),
            pltpu.VMEM((tiles, TILE, width), bf),
            pltpu.VMEM((tiles, TILE, width), bf),
            pltpu.VMEM((2, width, cols // 2), bf),
            pltpu.VMEM((tiles, 2, TILE, half), bf),
            pltpu.VMEM((2, TILE, half), bf),
            pltpu.VMEM((2, TILE, half), bf),
            pltpu.VMEM((2, 2, TILE // 2, half), bf),
            pltpu.VMEM((2, 2, TILE // 2, half), bf),
            pltpu.VMEM((2, TILE // 2, half), bf),
            dma((heads,)), dma, dma,
            dma((SPAN, FAR)), dma((SPAN, FAR)), dma((5,)), dma((5,)), dma, dma, dma((4,)), dma((4,)),
            dma((2,)), dma((2,)), dma((2, 2)), dma((2, 2)), dma((2, 2)), dma((2, 2)), dma, dma,
        ],
        compiler_params=pltpu.CompilerParams(
            collective_id=0, has_side_effects=True, vmem_limit_bytes=56 << 20
        ),
        cost_estimate=pl.CostEstimate(flops=8_000_000_000, bytes_accessed=8_000_000, transcendentals=6_000_000),
        name="attend_project",
    )(doc_lengths, queries.reshape(tiles, TILE, width), keys_values, out_weight)


def solution(mesh):
    placed = (P("ctx", "tp"), P(None, "ctx", "tp"), P(), P("tp", None))
    return jax.shard_map(
        on_device, mesh=mesh, in_specs=placed, out_specs=P(("ctx", "tp"), None), check_vma=False
    )
```

time: 137 us -> 59.5 us (0.43)
  the two profiles are of different devices: /device:TPU:8 before, /device:TPU:1 now
where the time goes in v1:
time: 59.5 us; the launch traced here: 59.4 us
  Pallas kernels  57.6 us (97%)
  local copies, waits for them, and re-layouts  1.72 us (3%)
    pallas_call x1, Pallas kernels, on_device(): pl.pallas_call(kernel, out_shape=jax.ShapeDtypeStruct((rows // n_tp, cols...  57.6 us
    unnamed x1, local copies, waits for them, and re-layouts  1.72 us

profile of v1, /device:TPU:1, one launch (start us, length us, event | category | flops | bytes accessed | tf_op | source)
XLA Modules:
  0.0 59.4 jit_solution(808956993861949608)
XLA Ops:
  0.0 57.6 %attend_project.1 = bf16[64,2560]{1,0:T(8,128)(2,1)} custom-call(s32[32]{0:T(128)} %doc_ref.1, bf16[4,128,640]{2,1,0:T(8,128)(2,1)} %bitcast.1, bf16[2,512,128]{2,1,0:T(8,128)(2,1)} %kv_hbm.1, bf16[640,2560]{1,0:T(8,128)(2,1)} %w_hbm.1), custom_call_target="tpu_custom_call" | custom-call | flops 8000000000 | bytes 8000000 | tf_op jit(solution)/shard_map/attend_project/pallas_call | solution.py:327
  57.6 1.7 %copy.6 = bf16[64,2560]{1,0:T(8,128)(2,1)} copy(bf16[64,2560]{1,0:T(8,128)(2,1)} %attend_project.1) | data formatting | bytes 655360

commit v2 on v1

--- a/solution.py
+++ b/solution.py
@@ -13,14 +13,15 @@
 LOW = -(2.0**100)
 LOGICAL = pl.DeviceIdType.MESH
 FAR = 3
+PART = TILE // 2
 
 
 def kernel(
     doc_ref, q_hbm, kv_hbm, w_hbm, out_ref,
     qs, qe, ke, kvb, relay, top, acc, att, att_sib, wbuf, pbuf, step_in, fwd, near, last, mine,
     q_sem, kv_sem, w_sem,
-    up_send, up_recv, down_send, down_recv, w_send, w_recv, att_send, att_recv,
-    s1_send, s1_recv, near_send, near_recv, last_send, last_recv, mine_send, mine_recv,
+    up_send, up_recv, jump_send, jump_recv, down_send, down_recv, end_send, w_send, w_recv, att_send, att_recv,
+    s1_send, s1_recv, near_send, near_recv, last_send, last_recv, mine_send, mine_recv, ready,
 ):
     n_ctx = lax.axis_size("ctx")
     n_rows = kvb.shape[2]
@@ -35,17 +36,44 @@
     x1 = x + 1 - 2 * (x % 2)
     x2 = (x + 2) % 4
     x3 = 3 - x
-    up = (me + 1) % n_ctx
-    down = (me + n_ctx - 1) % n_ctx
-    jump = (me + 5) % n_ctx
-    back = (me + n_ctx - 5) % n_ctx
+    end_ctx = n_ctx - 1
     sib = x * 2 + 1 - core
 
+    def ahead(by):
+        return jnp.minimum(me + by, end_ctx), tp
+
+    def behind(by):
+        return jnp.maximum(me - by, 0), tp
+
     barrier = pltpu.get_barrier_semaphore()
-    friends = [(up, tp), (down, tp), (jump, tp), (back, tp), (me, sib)]
-    friends += [(me, x1 * 2 + k) for k in range(2)] + [(me, x3 * 2 + k) for k in range(2)]
-    for friend in friends:
-        pl.semaphore_signal(barrier, inc=1, device_id=friend, device_id_type=LOGICAL)
+
+    def tell(semaphore, who):
+        pl.semaphore_signal(semaphore, inc=1, device_id=who, device_id_type=LOGICAL)
+
+    def if_ahead(by):
+        return pl.when(me + by <= end_ctx)
+
+    def if_behind(by):
+        return pl.when(me >= by)
+
+    n_friends = 5
+    for by in range(1, SPAN + 2):
+
+        @if_ahead(by)
+        def _(by=by):
+            tell(barrier, ahead(by))
+
+        n_friends = n_friends + jnp.where(me >= by, 1, 0)
+
+    @if_behind(1)
+    def _():
+        tell(barrier, behind(1))
+
+    n_friends = n_friends + jnp.where(me < end_ctx, 1, 0)
+    tell(barrier, (me, sib))
+    for chip in (x1, x3):
+        for k in range(2):
+            tell(barrier, (me, chip * 2 + k))
 
     q_copies = [
         pltpu.make_async_copy(
@@ -73,13 +101,23 @@
 
     def up_copy(j, c):
         src = piece(kv_hbm if j == 1 else kvb.at[j - 1], c)
-        return remote(src, piece(kvb.at[j], c), up_send.at[j - 1, c], up_recv.at[j - 1, c], (up, tp))
-
-    def down_copy(j):
-        if j == 5:
-            return remote(piece(kv_hbm, FAR), relay, down_send.at[4], down_recv.at[4], (jump, tp))
-        src = relay if j == 4 else piece(kvb.at[j + 1], FAR)
-        return remote(src, piece(kvb.at[j], FAR), down_send.at[j - 1], down_recv.at[j - 1], (down, tp))
+        return remote(src, piece(kvb.at[j], c), up_send.at[j - 1, c], up_recv.at[j - 1, c], ahead(1))
+
+    def part(ref, e):
+        return ref.at[:, pl.ds(FAR * TILE + e * PART, PART), :]
+
+    def jump_copy(e):
+        return remote(part(kv_hbm, e), relay.at[e], jump_send.at[e], jump_recv.at[e], ahead(SPAN + 1))
+
+    def down_copy(j, e):
+        return remote(
+            relay.at[e], part(kvb.at[j], e), down_send.at[j - 2, e], down_recv.at[j - 2, e], behind(SPAN + 1 - j)
+        )
+
+    def end_copy(j, e):
+        return remote(
+            part(kv_hbm, e), part(kvb.at[j], e), end_send.at[j - 2, e], down_recv.at[j - 2, e], ahead(j)
+        )
 
     w_remote = remote(w_hbm.at[:, sib_cols], wbuf.at[1], w_send, w_recv, (me, sib))
 
@@ -100,31 +138,78 @@
     qe[...] = jnp.where(inside(0), 1.0, 0.0).astype(jnp.bfloat16).reshape(qe.shape)
     ke[0] = jnp.where(inside(0), 0.0, LOW).astype(jnp.bfloat16)
 
-    pl.semaphore_wait(barrier, len(friends))
-    ups, downs = {}, {}
-    order = list(range(FAR))[::-1]
-    for c in order:
-        ups[1, c] = up_copy(1, c)
-        ups[1, c].start()
-    downs[5] = down_copy(5)
-    downs[5].start()
-    w_remote.start()
+    for j in range(1, SPAN + 1):
+
+        @pl.when(me < j)
+        def _(j=j):
+            kvb[j] = jnp.zeros(kvb.shape[1:], kvb.dtype)
+
+    pl.semaphore_wait(barrier, n_friends)
+
+    def start_own(c):
+        @if_ahead(1)
+        def _():
+            up_copy(1, c).start()
+
+    start_own(FAR)
+
+    @if_behind(SPAN + 1)
+    def _():
+        tell(ready, behind(SPAN + 1))
+
+    for j in range(2, SPAN + 1):
+
+        @pl.when((me >= j) & (me - j + SPAN + 1 > end_ctx))
+        def _(j=j):
+            tell(ready, behind(j))
+
     w_copy.start()
+
+    def start_jump(e):
+        @if_ahead(SPAN + 1)
+        def _():
+            if e == 0:
+                pl.semaphore_wait(ready, 1)
+            jump_copy(e).start()
+
+        @pl.when(me + SPAN + 1 > end_ctx)
+        def _():
+            if e == 0:
+
+                @if_ahead(2)
+                def _():
+                    pl.semaphore_wait(ready, jnp.minimum(end_ctx - me, SPAN) - 1)
+
+            for j in range(2, SPAN + 1):
+
+                @if_ahead(j)
+                def _(j=j):
+                    end_copy(j, e).start()
 
     for j in range(1, SPAN + 1):
         ke[j] = jnp.where(inside(j), 0.0, LOW).astype(jnp.bfloat16)
 
     def got_up(j, c):
-        ups[j, c].wait_recv()
-        if j < SPAN:
-            ups[j + 1, c] = up_copy(j + 1, c)
-            ups[j + 1, c].start()
-
-    def got_down(j):
-        downs[j].wait_recv()
-        if j > 1:
-            downs[j - 1] = down_copy(j - 1)
-            downs[j - 1].start()
+        @if_behind(j)
+        def _():
+            up_copy(j, c).wait_recv()
+            if j < SPAN and c < FAR:
+
+                @if_ahead(1)
+                def _():
+                    up_copy(j + 1, c).start()
+
+    def got_jump(e):
+        @if_behind(SPAN + 1)
+        def _():
+            jump_copy(e).wait_recv()
+            for j in (2, 3, 4):
+                down_copy(j, e).start()
+
+    def got_down(j, e):
+        @if_behind(j)
+        def _():
+            down_copy(j, e).wait_recv()
 
     scale = math.log2(math.e) / math.sqrt(HEAD_DIM)
 
@@ -187,66 +272,74 @@
     kv_copy.wait()
     for c in q_copies:
         c.wait()
-    attend([(t, [(0, 0, (t + 1) * TILE)], True) for t in range(n_tiles)])
-
-    def block(n):
-        return [(n, 0, FAR * TILE), (5 - n, FAR * TILE, TILE)]
-
+    first = [(t, [(0, 0, (t + 1) * TILE)], True) for t in range(n_tiles)]
+    attend(first[:2])
+    start_own(2)
+    attend(first[2:3])
+    start_own(1)
+    attend(first[3:])
+    start_own(0)
+    w_remote.start()
+
+    def whole(n, rows):
+        return [(t, [(n, 0, rows)], False) for t in range(n_tiles)]
+
+    got_up(1, 3)
     got_up(1, 2)
+    start_jump(0)
     got_up(1, 1)
+    start_jump(1)
     got_up(1, 0)
-    got_down(5)
+    attend(whole(1, n_rows)[:2])
     got_up(2, 2)
-    got_down(4)
-    attend([(t, block(1), False) for t in (0, 1)])
+    attend(whole(1, n_rows)[2:])
     got_up(2, 1)
-    attend([(t, block(1), False) for t in (2, 3)])
+    got_jump(0)
     got_up(2, 0)
+    got_jump(1)
+    attend(whole(2, FAR * TILE)[:2])
     got_up(3, 2)
-    got_down(3)
-    attend([(t, block(2), False) for t in (0, 1)])
+    attend(whole(2, FAR * TILE)[2:])
     got_up(3, 1)
-    attend([(t, block(2), False) for t in (2, 3)])
     got_up(3, 0)
-    got_down(2)
-    attend([(t, block(3), False) for t in (0, 1)])
+    attend(whole(3, FAR * TILE)[:2])
     got_up(4, 2)
-    attend([(t, block(3), False) for t in (2, 3)])
+    attend(whole(3, FAR * TILE)[2:])
+    for e in range(2):
+        for j in (4, 3, 2):
+            got_down(j, e)
+    attend([(t, [(j, FAR * TILE, TILE) for j in (4, 3, 2)], False) for t in range(n_tiles)])
     got_up(4, 1)
-    got_down(1)
-    lasts = []
-    for t in (3, 2, 1, 0):
-        spans = [(1, FAR * TILE, TILE)]
-        first_row = max(t, 1) * TILE
-        if first_row < FAR * TILE:
-            spans = [(4, first_row, FAR * TILE - first_row)] + spans
-        lasts.append((t, spans, False))
-    attend(lasts)
+
+    def finish(t):
+        a = acc[t]
+        done = (a[:, :HEAD_DIM] / a[:, HEAD_DIM:]).astype(jnp.bfloat16)
+        for h in range(heads):
+            att[t, :, h * HEAD_DIM : (h + 1) * HEAD_DIM] = done[h * TILE : (h + 1) * TILE, :]
+        att_copy(t).start()
+
+    def att_copy(t):
+        return remote(att.at[t], att_sib.at[t], att_send.at[t], att_recv.at[t], (me, sib))
+
+    attend([(t, [(SPAN, max(t, 1) * TILE, (FAR - max(t, 1)) * TILE)], False) for t in (2, 1, 0)])
+    for t in (3, 2, 1):
+        finish(t)
     got_up(4, 0)
-    attend([(0, [(4, 0, TILE)], False)])
-
-    att_copies = {}
-    for place, t in enumerate((x2, x1, x3, x)):
-        a = acc[t]
-        whole = (a[:, :HEAD_DIM] / a[:, HEAD_DIM:]).astype(jnp.bfloat16)
-        for h in range(heads):
-            att[place, :, h * HEAD_DIM : (h + 1) * HEAD_DIM] = whole[h * TILE : (h + 1) * TILE, :]
-        att_copies[place] = remote(
-            att.at[place], att_sib.at[place], att_send.at[place], att_recv.at[place], (me, sib)
-        )
-        att_copies[place].start()
+    attend([(0, [(SPAN, 0, TILE)], False)])
+    finish(0)
 
     w_copy.wait()
     w_remote.wait()
     sends = []
 
     def project(place):
-        att_copies[place].wait()
+        t = (x2, x1, x3, x)[place]
+        att_copy(t).wait_recv()
         for side in range(2):
             cols = slice(side * half_cols, (side + 1) * half_cols)
-            part = jnp.dot(att[place], wbuf[0, :, cols], preferred_element_type=jnp.float32)
-            part = part + jnp.dot(att_sib[place], wbuf[1, :, cols], preferred_element_type=jnp.float32)
-            pbuf[place, side] = part.astype(jnp.bfloat16)
+            total = jnp.dot(att[t], wbuf[0, :, cols], preferred_element_type=jnp.float32)
+            total = total + jnp.dot(att_sib[t], wbuf[1, :, cols], preferred_element_type=jnp.float32)
+            pbuf[place, side] = total.astype(jnp.bfloat16)
 
     def send(copy):
         copy.start()
@@ -270,14 +363,15 @@
 
     project(0)
     hops = [
-        send(remote(pbuf.at[0, side], step_in.at[side], s1_send.at[side], s1_recv.at[side], (me, partner[side] * 2 + core)))
+        remote(pbuf.at[0, side], step_in.at[side], s1_send.at[side], s1_recv.at[side], (me, partner[side] * 2 + core))
         for side in range(2)
     ]
-    project(1)
+    for hop in hops:
+        hop.start()
+    for place in (1, 2, 3):
+        project(place)
     to_cores(pbuf.at[1, 0], near, near_send, near_recv, 0, x1)
-    project(2)
     to_cores(pbuf.at[2, 1], near, near_send, near_recv, 1, x3)
-    project(3)
     other = pl.multiple_of((1 - core) * rows_out, rows_out)
     own = pl.multiple_of(core * rows_out, rows_out)
     mine_copy = send(
@@ -285,6 +379,7 @@
     )
     for side in range(2):
         hops[side].wait_recv()
+        sends.append(hops[side])
         held = pbuf[2 - side, side].astype(jnp.float32) + step_in[side].astype(jnp.float32)
         fwd[side] = held.astype(jnp.bfloat16)
         to_cores(fwd.at[side], last, last_send, last_recv, side, partner[1 - side])
@@ -308,10 +403,39 @@
 
     for copy in sends:
         copy.wait_send()
-    for copy in ups.values():
-        copy.wait_send()
-    for copy in downs.values():
-        copy.wait_send()
+    for t in range(n_tiles):
+        att_copy(t).wait_send()
+
+    @if_ahead(1)
+    def _():
+        for c in range(FAR + 1):
+            up_copy(1, c).wait_send()
+        for j in range(2, SPAN + 1):
+
+            @if_behind(j - 1)
+            def _(j=j):
+                for c in range(FAR):
+                    up_copy(j, c).wait_send()
+
+    @if_ahead(SPAN + 1)
+    def _():
+        for e in range(2):
+            jump_copy(e).wait_send()
+
+    @if_behind(SPAN + 1)
+    def _():
+        for e in range(2):
+            for j in (2, 3, 4):
+                down_copy(j, e).wait_send()
+
+    @pl.when(me + SPAN + 1 > end_ctx)
+    def _():
+        for j in range(2, SPAN + 1):
+
+            @if_ahead(j)
+            def _(j=j):
+                for e in range(2):
+                    end_copy(j, e).wait_send()
 
 
 def on_device(queries, keys_values, doc_lengths, out_weight):
@@ -334,7 +458,7 @@
             pltpu.VMEM((tiles, TILE, 128), bf),
             pltpu.VMEM((SPAN + 1, rows, 128), bf),
             pltpu.VMEM((SPAN + 1, 2, rows, HEAD_DIM), bf),
-            pltpu.VMEM((2, TILE, HEAD_DIM), bf),
+            pltpu.VMEM((2, 2, PART, HEAD_DIM), bf),
             pltpu.VMEM((tiles, heads * TILE, 128), f32),
             pltpu.VMEM((tiles, heads * TILE, 2 * HEAD_DIM), f32),
             pltpu.VMEM((tiles, TILE, width), bf),
@@ -347,8 +471,9 @@
             pltpu.VMEM((2, 2, TILE // 2, half), bf),
             pltpu.VMEM((2, TILE // 2, half), bf),
             dma((heads,)), dma, dma,
-            dma((SPAN, FAR)), dma((SPAN, FAR)), dma((5,)), dma((5,)), dma, dma, dma((4,)), dma((4,)),
+            dma((SPAN, FAR + 1)), dma((SPAN, FAR + 1)), dma((2,)), dma((2,)), dma((SPAN - 1, 2)), dma((SPAN - 1, 2)), dma((SPAN - 1, 2)), dma, dma, dma((4,)), dma((4,)),
             dma((2,)), dma((2,)), dma((2, 2)), dma((2, 2)), dma((2, 2)), dma((2, 2)), dma, dma,
+            pltpu.SemaphoreType.REGULAR,
         ],
         compiler_params=pltpu.CompilerParams(
             collective_id=0, has_side_effects=True, vmem_limit_bytes=56 << 20

time: 59.5 us -> 51.5 us (0.87)
  the two profiles are of different devices: /device:TPU:1 before, /device:TPU:497 now
where the time goes in v2:
time: 51.5 us; the launch traced here: 51.4 us
  Pallas kernels  49.6 us (96%)
  local copies, waits for them, and re-layouts  1.72 us (3%)
    pallas_call x1, Pallas kernels, on_device(): pl.pallas_call(kernel, out_shape=jax.ShapeDtypeStruct((rows // n_tp, cols...  49.6 us
    unnamed x1, local copies, waits for them, and re-layouts  1.72 us

profile of v2, /device:TPU:497, one launch (start us, length us, event | category | flops | bytes accessed | tf_op | source)
XLA Modules:
  0.0 51.4 jit_solution(16209368370079995507)
XLA Ops:
  0.0 49.6 %attend_project.1 = bf16[64,2560]{1,0:T(8,128)(2,1)} custom-call(s32[32]{0:T(128)} %doc_ref.1, bf16[4,128,640]{2,1,0:T(8,128)(2,1)} %bitcast.1, bf16[2,512,128]{2,1,0:T(8,128)(2,1)} %kv_hbm.1, bf16[640,2560]{1,0:T(8,128)(2,1)} %w_hbm.1), custom_call_target="tpu_custom_call" | custom-call | flops 8000000000 | bytes 8000000 | tf_op jit(solution)/shard_map/attend_project/pallas_call | solution.py:451
  49.6 1.7 %copy.6 = bf16[64,2560]{1,0:T(8,128)(2,1)} copy(bf16[64,2560]{1,0:T(8,128)(2,1)} %attend_project.1) | data formatting | bytes 655360

commit v3 on v2

--- a/solution.py
+++ b/solution.py
@@ -17,9 +17,9 @@
 
 
 def kernel(
-    doc_ref, q_hbm, kv_hbm, w_hbm, out_ref,
-    qs, qe, ke, kvb, relay, top, acc, att, att_sib, wbuf, pbuf, step_in, fwd, near, last, mine,
-    q_sem, kv_sem, w_sem,
+    doc_hbm, q_hbm, kv_hbm, w_hbm, sum_hbm, last_hbm,
+    qs, qe, ke, kvb, relay, top, acc, att, att_sib, wbuf, pbuf, step_in, fwd, near, sums, mine, doc_ref,
+    doc_sem, q_sem, kv_sem, w_sem, sum_sem,
     up_send, up_recv, jump_send, jump_recv, down_send, down_recv, end_send, w_send, w_recv, att_send, att_recv,
     s1_send, s1_recv, near_send, near_recv, last_send, last_recv, mine_send, mine_recv, ready,
 ):
@@ -45,6 +45,8 @@
     def behind(by):
         return jnp.maximum(me - by, 0), tp
 
+    doc_copy = pltpu.make_async_copy(doc_hbm, doc_ref, doc_sem)
+    doc_copy.start()
     barrier = pltpu.get_barrier_semaphore()
 
     def tell(semaphore, who):
@@ -121,6 +123,7 @@
 
     w_remote = remote(w_hbm.at[:, sib_cols], wbuf.at[1], w_send, w_recv, (me, sib))
 
+    doc_copy.wait()
     lane = lax.broadcasted_iota(jnp.int32, (1, 128), 1)
     low_end = jnp.zeros((1, 128), jnp.int32)
     high_end = jnp.zeros((1, 128), jnp.int32)
@@ -279,36 +282,41 @@
     start_own(1)
     attend(first[3:])
     start_own(0)
-    w_remote.start()
+    start_jump(0)
 
     def whole(n, rows):
         return [(t, [(n, 0, rows)], False) for t in range(n_tiles)]
 
     got_up(1, 3)
+    start_jump(1)
     got_up(1, 2)
-    start_jump(0)
     got_up(1, 1)
-    start_jump(1)
+    got_jump(0)
     got_up(1, 0)
+    got_jump(1)
     attend(whole(1, n_rows)[:2])
     got_up(2, 2)
     attend(whole(1, n_rows)[2:])
+    w_remote.start()
     got_up(2, 1)
-    got_jump(0)
     got_up(2, 0)
-    got_jump(1)
     attend(whole(2, FAR * TILE)[:2])
     got_up(3, 2)
     attend(whole(2, FAR * TILE)[2:])
     got_up(3, 1)
     got_up(3, 0)
     attend(whole(3, FAR * TILE)[:2])
+    attend(whole(3, FAR * TILE)[2:])
+
+    def ends(*blocks):
+        for j in blocks:
+            for e in range(2):
+                got_down(j, e)
+        return [(j, FAR * TILE, TILE) for j in blocks]
+
+    spans = ends(4, 3)
+    attend([(t, spans, False) for t in range(n_tiles)])
     got_up(4, 2)
-    attend(whole(3, FAR * TILE)[2:])
-    for e in range(2):
-        for j in (4, 3, 2):
-            got_down(j, e)
-    attend([(t, [(j, FAR * TILE, TILE) for j in (4, 3, 2)], False) for t in range(n_tiles)])
     got_up(4, 1)
 
     def finish(t):
@@ -321,7 +329,14 @@
     def att_copy(t):
         return remote(att.at[t], att_sib.at[t], att_send.at[t], att_recv.at[t], (me, sib))
 
-    attend([(t, [(SPAN, max(t, 1) * TILE, (FAR - max(t, 1)) * TILE)], False) for t in (2, 1, 0)])
+    spans = ends(2)
+    starts = {t: max(t, 1) * TILE for t in (3, 2, 1, 0)}
+    attend(
+        [
+            (t, ([(SPAN, r, FAR * TILE - r)] if r < FAR * TILE else []) + spans, False)
+            for t, r in starts.items()
+        ]
+    )
     for t in (3, 2, 1):
         finish(t)
     got_up(4, 0)
@@ -334,11 +349,11 @@
 
     def project(place):
         t = (x2, x1, x3, x)[place]
+        sides = [slice(side * half_cols, (side + 1) * half_cols) for side in range(2)]
+        totals = [jnp.dot(att[t], wbuf[0, :, cols], preferred_element_type=jnp.float32) for cols in sides]
         att_copy(t).wait_recv()
-        for side in range(2):
-            cols = slice(side * half_cols, (side + 1) * half_cols)
-            total = jnp.dot(att[t], wbuf[0, :, cols], preferred_element_type=jnp.float32)
-            total = total + jnp.dot(att_sib[t], wbuf[1, :, cols], preferred_element_type=jnp.float32)
+        for side, cols in enumerate(sides):
+            total = totals[side] + jnp.dot(att_sib[t], wbuf[1, :, cols], preferred_element_type=jnp.float32)
             pbuf[place, side] = total.astype(jnp.bfloat16)
 
     def send(copy):
@@ -348,13 +363,16 @@
 
     rows_out = TILE // 2
     partner = (x1, x3)
+
+    def last_piece(k, side):
+        return last_hbm.at[:, pl.ds(pl.multiple_of((2 * k + side) * half_cols, 128), half_cols)]
 
     def to_cores(src, dst, send_sem, recv_sem, side, chip):
         for k in range(2):
             send(
                 remote(
                     src.at[pl.ds(k * rows_out, rows_out), :],
-                    dst.at[core, side],
+                    dst,
                     send_sem.at[side, k],
                     recv_sem.at[core, side],
                     (me, chip * 2 + k),
@@ -370,8 +388,8 @@
         hop.start()
     for place in (1, 2, 3):
         project(place)
-    to_cores(pbuf.at[1, 0], near, near_send, near_recv, 0, x1)
-    to_cores(pbuf.at[2, 1], near, near_send, near_recv, 1, x3)
+    to_cores(pbuf.at[1, 0], near.at[core, 0], near_send, near_recv, 0, x1)
+    to_cores(pbuf.at[2, 1], near.at[core, 1], near_send, near_recv, 1, x3)
     other = pl.multiple_of((1 - core) * rows_out, rows_out)
     own = pl.multiple_of(core * rows_out, rows_out)
     mine_copy = send(
@@ -382,24 +400,26 @@
         sends.append(hops[side])
         held = pbuf[2 - side, side].astype(jnp.float32) + step_in[side].astype(jnp.float32)
         fwd[side] = held.astype(jnp.bfloat16)
-        to_cores(fwd.at[side], last, last_send, last_recv, side, partner[1 - side])
-
-    def arrived(buf, sems_s, sems_r, k, side):
-        remote(buf.at[k, side], buf.at[k, side], sems_s.at[side, 0], sems_r.at[k, side], (me, sib)).wait_recv()
+        to_cores(fwd.at[side], last_piece(core, side), last_send, last_recv, side, partner[1 - side])
+
+    def arrived(dst, sems_s, sems_r, k, side):
+        remote(near.at[k, side], dst, sems_s.at[side, 0], sems_r.at[k, side], (me, sib)).wait_recv()
 
     mine_copy.wait_recv()
     for k in range(2):
         for side in range(2):
-            arrived(near, near_send, near_recv, k, side)
-    for side in range(2):
-        for k in range(2):
-            arrived(last, last_send, last_recv, k, side)
+            arrived(near.at[k, side], near_send, near_recv, k, side)
             here = pbuf[3, side, pl.ds(own, rows_out), :].astype(jnp.float32)
             there = mine[side].astype(jnp.float32)
             base = jnp.where(core == k, here, there)
-            total = base + near[k, side].astype(jnp.float32) + last[k, side].astype(jnp.float32)
             col = (2 * k + side) * half_cols
-            out_ref[:, col : col + half_cols] = total.astype(jnp.bfloat16)
+            sums[:, col : col + half_cols] = base + near[k, side].astype(jnp.float32)
+    sum_copy = pltpu.make_async_copy(sums, sum_hbm, sum_sem)
+    sum_copy.start()
+    for k in range(2):
+        for side in range(2):
+            arrived(last_piece(k, side), last_send, last_recv, k, side)
+    sum_copy.wait()
 
     for copy in sends:
         copy.wait_send()
@@ -448,11 +468,11 @@
     bf, f32 = jnp.bfloat16, jnp.float32
     dma = pltpu.SemaphoreType.DMA
     hbm = pl.BlockSpec(memory_space=pl.ANY)
-    return pl.pallas_call(
+    sums, lasts = pl.pallas_call(
         kernel,
-        out_shape=jax.ShapeDtypeStruct((rows // n_tp, cols), bf),
-        in_specs=[pl.BlockSpec(memory_space=pltpu.SMEM), hbm, hbm, hbm],
-        out_specs=pl.BlockSpec(memory_space=pltpu.VMEM),
+        out_shape=[jax.ShapeDtypeStruct((rows // n_tp, cols), kind) for kind in (f32, bf)],
+        in_specs=[hbm, hbm, hbm, hbm],
+        out_specs=[hbm, hbm],
         scratch_shapes=[
             pltpu.VMEM((tiles, heads * TILE, HEAD_DIM), bf),
             pltpu.VMEM((tiles, TILE, 128), bf),
@@ -468,19 +488,26 @@
             pltpu.VMEM((2, TILE, half), bf),
             pltpu.VMEM((2, TILE, half), bf),
             pltpu.VMEM((2, 2, TILE // 2, half), bf),
-            pltpu.VMEM((2, 2, TILE // 2, half), bf),
+            pltpu.VMEM((TILE // 2, cols), f32),
             pltpu.VMEM((2, TILE // 2, half), bf),
-            dma((heads,)), dma, dma,
+            pltpu.SMEM(doc_lengths.shape, jnp.int32),
+            dma, dma((heads,)), dma, dma, dma,
             dma((SPAN, FAR + 1)), dma((SPAN, FAR + 1)), dma((2,)), dma((2,)), dma((SPAN - 1, 2)), dma((SPAN - 1, 2)), dma((SPAN - 1, 2)), dma, dma, dma((4,)), dma((4,)),
             dma((2,)), dma((2,)), dma((2, 2)), dma((2, 2)), dma((2, 2)), dma((2, 2)), dma, dma,
             pltpu.SemaphoreType.REGULAR,
         ],
         compiler_params=pltpu.CompilerParams(
-            collective_id=0, has_side_effects=True, vmem_limit_bytes=56 << 20
+            collective_id=0, has_side_effects=True, vmem_limit_bytes=40 << 20
         ),
         cost_estimate=pl.CostEstimate(flops=8_000_000_000, bytes_accessed=8_000_000, transcendentals=6_000_000),
         name="attend_project",
-    )(doc_lengths, queries.reshape(tiles, TILE, width), keys_values, out_weight)
+    )(
+        *(
+            pltpu.with_memory_space_constraint(a, pltpu.HBM)
+            for a in (doc_lengths, queries.reshape(tiles, TILE, width), keys_values, out_weight)
+        )
+    )
+    return (sums + lasts.astype(f32)).astype(bf)
 
 
 def solution(mesh):

time: 51.5 us -> 47.9 us (0.930)
  Pallas kernels: 49.6 us -> 47 us
  local copies, waits for them, and re-layouts: 1.72 us -> 0 us
  other arithmetic: 0 us -> 0.78 us
    pallas_call x1, Pallas kernels: 49.6 us -> 47 us  [on_device(): pl.pallas_call(kernel, out_shape=[jax.ShapeDtypeStruct((rows // n_tp, col...]
    unnamed x1 -> x0, local copies, waits for them, and re-layouts: 1.72 us -> none
    convert_element_type x0 -> x1, other arithmetic: none -> 0.78 us  [on_device(): return (sums + lasts.astype(f32)).astype(bf)]
where the time goes in v3:
time: 47.9 us; the launch traced here: 47.8 us
  Pallas kernels  47 us (98%)
  other arithmetic  0.78 us (2%)
    pallas_call x1, Pallas kernels, on_device(): pl.pallas_call(kernel, out_shape=[jax.ShapeDtypeStruct((rows // n_tp, col...  47 us

profile of v3, /device:TPU:497, one launch (start us, length us, event | category | flops | bytes accessed | tf_op | source)
XLA Modules:
  0.0 47.8 jit_solution(7434522539242682411)
XLA Ops:
  0.0 47.0 %attend_project.1 = (f32[64,2560]{1,0:T(8,128)S(1)}, bf16[64,2560]{1,0:T(8,128)(2,1)S(1)}) custom-call(s32[32]{0:T(128)} %doc_hbm.1, bf16[4,128,640]{2,1,0:T(8,128)(2,1)} %bitcast.1, bf16[2,512,128]{2,1,0:T(8,128)(2,1)} %kv_hbm.1, bf16[640,2560]{1,0:T(8,128)(2,1)} %w_hbm.1), custom_call_target="tpu_custom_call" | custom-call | flops 8000000000 | bytes 8000000 | tf_op jit(solution)/shard_map/attend_project/pallas_call | solution.py:471
  47.0 0.8 %add_convert_fusion = bf16[64,2560]{1,0:T(8,128)(2,1)} fusion(f32[64,2560]{1,0:T(8,128)S(1)} %get-tuple-element.7, bf16[64,2560]{1,0:T(8,128)(2,1)S(1)} %get-tuple-element.8), kind=kLoop, calls=%fused_computation | loop fusion | flops 491520 | bytes 1310720 | tf_op jit(solution)/shard_map/convert_element_type | solution.py:510

commit v4 on v3

--- a/solution.py
+++ b/solution.py
@@ -123,6 +123,27 @@
 
     w_remote = remote(w_hbm.at[:, sib_cols], wbuf.at[1], w_send, w_recv, (me, sib))
 
+    pl.semaphore_wait(barrier, n_friends)
+
+    def start_own(c):
+        @if_ahead(1)
+        def _():
+            up_copy(1, c).start()
+
+    start_own(FAR)
+
+    @if_behind(SPAN + 1)
+    def _():
+        tell(ready, behind(SPAN + 1))
+
+    for j in range(2, SPAN + 1):
+
+        @pl.when((me >= j) & (me - j + SPAN + 1 > end_ctx))
+        def _(j=j):
+            tell(ready, behind(j))
+
+    w_copy.start()
+
     doc_copy.wait()
     lane = lax.broadcasted_iota(jnp.int32, (1, 128), 1)
     low_end = jnp.zeros((1, 128), jnp.int32)
@@ -147,26 +168,7 @@
         def _(j=j):
             kvb[j] = jnp.zeros(kvb.shape[1:], kvb.dtype)
 
-    pl.semaphore_wait(barrier, n_friends)
-
-    def start_own(c):
-        @if_ahead(1)
-        def _():
-            up_copy(1, c).start()
-
-    start_own(FAR)
-
-    @if_behind(SPAN + 1)
-    def _():
-        tell(ready, behind(SPAN + 1))
-
-    for j in range(2, SPAN + 1):
-
-        @pl.when((me >= j) & (me - j + SPAN + 1 > end_ctx))
-        def _(j=j):
-            tell(ready, behind(j))
-
-    w_copy.start()
+    start_own(2)
 
     def start_jump(e):
         @if_ahead(SPAN + 1)
@@ -260,7 +262,7 @@
         else:
             acc[t] = acc[t] * jnp.concatenate([factor, factor], axis=1) + part
 
-    def attend(items):
+    def attend(items, then=None):
         held = scores(items[0])
         pending = None
         for i, item in enumerate(items):
@@ -268,20 +270,22 @@
             now = soften(item, held)
             if pending is not None:
                 gather(*pending)
+                if then is not None:
+                    then(pending[0][0])
             pending = (item, *now)
             held = following
         gather(*pending)
+        if then is not None:
+            then(pending[0][0])
 
     kv_copy.wait()
     for c in q_copies:
         c.wait()
     first = [(t, [(0, 0, (t + 1) * TILE)], True) for t in range(n_tiles)]
+    start_own(1)
     attend(first[:2])
-    start_own(2)
-    attend(first[2:3])
-    start_own(1)
-    attend(first[3:])
     start_own(0)
+    attend(first[2:])
     start_jump(0)
 
     def whole(n, rows):
@@ -315,9 +319,10 @@
         return [(j, FAR * TILE, TILE) for j in blocks]
 
     spans = ends(4, 3)
-    attend([(t, spans, False) for t in range(n_tiles)])
     got_up(4, 2)
+    attend([(t, ([(SPAN, 2 * TILE, TILE)] if t < 3 else []) + spans, False) for t in range(n_tiles)])
     got_up(4, 1)
+    got_up(4, 0)
 
     def finish(t):
         a = acc[t]
@@ -330,18 +335,10 @@
         return remote(att.at[t], att_sib.at[t], att_send.at[t], att_recv.at[t], (me, sib))
 
     spans = ends(2)
-    starts = {t: max(t, 1) * TILE for t in (3, 2, 1, 0)}
     attend(
-        [
-            (t, ([(SPAN, r, FAR * TILE - r)] if r < FAR * TILE else []) + spans, False)
-            for t, r in starts.items()
-        ]
+        [(t, ([(SPAN, t * TILE, (2 - t) * TILE)] if t < 2 else []) + spans, False) for t in range(n_tiles)],
+        finish,
     )
-    for t in (3, 2, 1):
-        finish(t)
-    got_up(4, 0)
-    attend([(0, [(SPAN, 0, TILE)], False)])
-    finish(0)
 
     w_copy.wait()
     w_remote.wait()
@@ -367,40 +364,52 @@
     def last_piece(k, side):
         return last_hbm.at[:, pl.ds(pl.multiple_of((2 * k + side) * half_cols, 128), half_cols)]
 
-    def to_cores(src, dst, send_sem, recv_sem, side, chip):
-        for k in range(2):
-            send(
-                remote(
-                    src.at[pl.ds(k * rows_out, rows_out), :],
-                    dst,
-                    send_sem.at[side, k],
-                    recv_sem.at[core, side],
-                    (me, chip * 2 + k),
-                )
+    def to_core(src, dst, send_sem, recv_sem, side, chip, k):
+        send(
+            remote(
+                src.at[pl.ds(k * rows_out, rows_out), :],
+                dst,
+                send_sem.at[side, k],
+                recv_sem.at[core, side],
+                (me, chip * 2 + k),
             )
-
-    project(0)
-    hops = [
-        remote(pbuf.at[0, side], step_in.at[side], s1_send.at[side], s1_recv.at[side], (me, partner[side] * 2 + core))
-        for side in range(2)
-    ]
-    for hop in hops:
-        hop.start()
-    for place in (1, 2, 3):
+        )
+
+    def hop(side, k):
+        rows_k = pl.ds(k * rows_out, rows_out)
+        return remote(
+            pbuf.at[0, side, rows_k, :],
+            step_in.at[side, rows_k, :],
+            s1_send.at[side, k],
+            s1_recv.at[side, k],
+            (me, partner[side] * 2 + core),
+        )
+
+    for place, k in enumerate((1, 0)):
         project(place)
-    to_cores(pbuf.at[1, 0], near.at[core, 0], near_send, near_recv, 0, x1)
-    to_cores(pbuf.at[2, 1], near.at[core, 1], near_send, near_recv, 1, x3)
+        for side in range(2):
+            send(hop(side, k))
+    project(2)
+    project(3)
     other = pl.multiple_of((1 - core) * rows_out, rows_out)
     own = pl.multiple_of(core * rows_out, rows_out)
     mine_copy = send(
         remote(pbuf.at[3, :, pl.ds(other, rows_out), :], mine, mine_send, mine_recv, (me, sib))
     )
-    for side in range(2):
-        hops[side].wait_recv()
-        sends.append(hops[side])
-        held = pbuf[2 - side, side].astype(jnp.float32) + step_in[side].astype(jnp.float32)
-        fwd[side] = held.astype(jnp.bfloat16)
-        to_cores(fwd.at[side], last_piece(core, side), last_send, last_recv, side, partner[1 - side])
+    for half in (1,):
+        to_core(pbuf.at[1, 0], near.at[core, 0], near_send, near_recv, 0, x1, half)
+        to_core(pbuf.at[2, 1], near.at[core, 1], near_send, near_recv, 1, x3, half)
+    for k in (1, 0):
+        rows_k = slice(k * rows_out, (k + 1) * rows_out)
+        for side in range(2):
+            hop(side, k).wait_recv()
+            held = pbuf[2 - side, side, rows_k, :].astype(jnp.float32) + step_in[side, rows_k, :].astype(jnp.float32)
+            fwd[side, rows_k, :] = held.astype(jnp.bfloat16)
+            to_core(fwd.at[side], last_piece(core, side), last_send, last_recv, side, partner[1 - side], k)
+        if k == 1:
+            for half in (0,):
+                to_core(pbuf.at[1, 0], near.at[core, 0], near_send, near_recv, 0, x1, half)
+                to_core(pbuf.at[2, 1], near.at[core, 1], near_send, near_recv, 1, x3, half)
 
     def arrived(dst, sems_s, sems_r, k, side):
         remote(near.at[k, side], dst, sems_s.at[side, 0], sems_r.at[k, side], (me, sib)).wait_recv()
@@ -493,7 +502,7 @@
             pltpu.SMEM(doc_lengths.shape, jnp.int32),
             dma, dma((heads,)), dma, dma, dma,
             dma((SPAN, FAR + 1)), dma((SPAN, FAR + 1)), dma((2,)), dma((2,)), dma((SPAN - 1, 2)), dma((SPAN - 1, 2)), dma((SPAN - 1, 2)), dma, dma, dma((4,)), dma((4,)),
-            dma((2,)), dma((2,)), dma((2, 2)), dma((2, 2)), dma((2, 2)), dma((2, 2)), dma, dma,
+            dma((2, 2)), dma((2, 2)), dma((2, 2)), dma((2, 2)), dma((2, 2)), dma((2, 2)), dma, dma,
             pltpu.SemaphoreType.REGULAR,
         ],
         compiler_params=pltpu.CompilerParams(

time: 47.9 us -> 47.9 us (level)
  the two profiles are of different devices: /device:TPU:497 before, /device:TPU:504 now
where the time goes in v4:
time: 47.9 us; the launch traced here: 47.8 us
  Pallas kernels  47 us (98%)
  other arithmetic  0.78 us (2%)
    pallas_call x1, Pallas kernels, on_device(): pl.pallas_call(kernel, out_shape=[jax.ShapeDtypeStruct((rows // n_tp, col...  47 us

profile of v4, /device:TPU:504, one launch (start us, length us, event | category | flops | bytes accessed | tf_op | source)
XLA Modules:
  0.0 47.8 jit_solution(12015275376916095791)
XLA Ops:
  0.0 47.0 %attend_project.1 = (f32[64,2560]{1,0:T(8,128)S(1)}, bf16[64,2560]{1,0:T(8,128)(2,1)S(1)}) custom-call(s32[32]{0:T(128)} %doc_hbm.1, bf16[4,128,640]{2,1,0:T(8,128)(2,1)} %bitcast.1, bf16[2,512,128]{2,1,0:T(8,128)(2,1)} %kv_hbm.1, bf16[640,2560]{1,0:T(8,128)(2,1)} %w_hbm.1), custom_call_target="tpu_custom_call" | custom-call | flops 8000000000 | bytes 8000000 | tf_op jit(solution)/shard_map/attend_project/pallas_call | solution.py:480
  47.0 0.8 %add_convert_fusion = bf16[64,2560]{1,0:T(8,128)(2,1)} fusion(f32[64,2560]{1,0:T(8,128)S(1)} %get-tuple-element.7, bf16[64,2560]{1,0:T(8,128)(2,1)S(1)} %get-tuple-element.8), kind=kLoop, calls=%fused_computation | loop fusion | flops 491520 | bytes 1310720 | tf_op jit(solution)/shard_map/convert_element_type | solution.py:519

commit v5 on v4

--- a/solution.py
+++ b/solution.py
@@ -385,10 +385,11 @@
             (me, partner[side] * 2 + core),
         )
 
-    for place, k in enumerate((1, 0)):
-        project(place)
+    project(0)
+    for k in range(2):
         for side in range(2):
             send(hop(side, k))
+    project(1)
     project(2)
     project(3)
     other = pl.multiple_of((1 - core) * rows_out, rows_out)
@@ -396,7 +397,7 @@
     mine_copy = send(
         remote(pbuf.at[3, :, pl.ds(other, rows_out), :], mine, mine_send, mine_recv, (me, sib))
     )
-    for half in (1,):
+    for half in (1, 0):
         to_core(pbuf.at[1, 0], near.at[core, 0], near_send, near_recv, 0, x1, half)
         to_core(pbuf.at[2, 1], near.at[core, 1], near_send, near_recv, 1, x3, half)
     for k in (1, 0):
@@ -406,10 +407,6 @@
             held = pbuf[2 - side, side, rows_k, :].astype(jnp.float32) + step_in[side, rows_k, :].astype(jnp.float32)
             fwd[side, rows_k, :] = held.astype(jnp.bfloat16)
             to_core(fwd.at[side], last_piece(core, side), last_send, last_recv, side, partner[1 - side], k)
-        if k == 1:
-            for half in (0,):
-                to_core(pbuf.at[1, 0], near.at[core, 0], near_send, near_recv, 0, x1, half)
-                to_core(pbuf.at[2, 1], near.at[core, 1], near_send, near_recv, 1, x3, half)
 
     def arrived(dst, sems_s, sems_r, k, side):
         remote(near.at[k, side], dst, sems_s.at[side, 0], sems_r.at[k, side], (me, sib)).wait_recv()

time: 47.9 us -> 47.9 us (level)
  no operation moved by 1% of the time
where the time goes in v5:
time: 47.9 us; the launch traced here: 47.8 us
  Pallas kernels  47 us (98%)
  other arithmetic  0.78 us (2%)
    pallas_call x1, Pallas kernels, on_device(): pl.pallas_call(kernel, out_shape=[jax.ShapeDtypeStruct((rows // n_tp, col...  47 us

profile of v5, /device:TPU:504, one launch (start us, length us, event | category | flops | bytes accessed | tf_op | source)
XLA Modules:
  0.0 47.8 jit_solution(15027207597281597933)
XLA Ops:
  0.0 47.0 %attend_project.1 = (f32[64,2560]{1,0:T(8,128)S(1)}, bf16[64,2560]{1,0:T(8,128)(2,1)S(1)}) custom-call(s32[32]{0:T(128)} %doc_hbm.1, bf16[4,128,640]{2,1,0:T(8,128)(2,1)} %bitcast.1, bf16[2,512,128]{2,1,0:T(8,128)(2,1)} %kv_hbm.1, bf16[640,2560]{1,0:T(8,128)(2,1)} %w_hbm.1), custom_call_target="tpu_custom_call" | custom-call | flops 8000000000 | bytes 8000000 | tf_op jit(solution)/shard_map/attend_project/pallas_call | solution.py:477
  47.0 0.8 %add_convert_fusion = bf16[64,2560]{1,0:T(8,128)(2,1)} fusion(f32[64,2560]{1,0:T(8,128)S(1)} %get-tuple-element.7, bf16[64,2560]{1,0:T(8,128)(2,1)S(1)} %get-tuple-element.8), kind=kLoop, calls=%fused_computation | loop fusion | flops 491520 | bytes 1310720 | tf_op jit(solution)/shard_map/convert_element_type | solution.py:516
